TPU v7x, 32 devices: a whole 2x2x4 slice. The times are simulated.
32 devices in a mesh: groups: 2 (over y), seq: 4 (over z), dp: 4 (over x, core).
Axes of the slice: x: 2, y: 2, z: 4, core: 2. Of those that a mesh axis runs over, the one named last changes fastest.
Arguments:
- query: bfloat16 [8, 512, 4096], P(('groups', 'dp'), 'seq'), parts along dimension 0
- key: bfloat16 [8, 512, 4096], P(('groups', 'dp'), 'seq'), parts along dimension 0
- value: bfloat16 [8, 512, 4096], P(('groups', 'dp'), 'seq'), parts along dimension 0, may hold values from -6 to 6
- grad_out: bfloat16 [8, 512, 4096], P(('groups', 'dp'), 'seq'), parts along dimension 0, may hold values from -6 to 6
- layout: int32 [32, 4, 4], replicated, may hold values from 0 to 1, as said below
- log_scale: float32 [32], replicated, may hold values from -0.3 to 0.3
Outputs:
- attended: bfloat16 [8, 512, 4096], P(('groups', 'dp'), 'seq'), parts along dimension 0
- grad_query: bfloat16 [8, 512, 4096], P(('groups', 'dp'), 'seq'), parts along dimension 0
- grad_key: bfloat16 [8, 512, 4096], P(('groups', 'dp'), 'seq'), parts along dimension 0
- grad_value: bfloat16 [8, 512, 4096], P(('groups', 'dp'), 'seq'), parts along dimension 0
- grad_log_scale: float32 [64], P('groups'), parts along dimension 0
There are 2 independent parts, one for each index of `groups`. A program takes and returns all parts, laid end to end along the dimension named above; an argument that names none is the same for every part. Nothing has to cross between parts.
Inputs may be any that keep to these rules, and one draw needn't show every extreme that they name: layout is 0 above the block diagonal and 1 on the block diagonal and in the first block column; heads differ widely in their density of open blocks.
All inputs are finite; a program needn't handle non-finite values.
Results may differ from a plain program's by a relative error of at most 0.02.
Values may be sent and summed in bfloat16 or wider, within the bound.
A program may use at most 128 MiB of HBM per device.

v0:
```python
import functools
import math

import jax
import jax.numpy as jnp
from jax import lax
from jax.experimental import pallas as pl
from jax.experimental.pallas import tpu as pltpu
from jax.sharding import PartitionSpec as P

HEADS = 32
HD = 128
BLK = 128


BIG_NEG = -1e30


def tile_scores(q_rows, k_tile, lay_sub, q_start, k_start, scale):
    rows = q_rows.shape[0]
    cols = k_tile.shape[0]
    scores = jnp.einsum("qd,kd->qk", q_rows, k_tile, preferred_element_type=jnp.float32) * scale
    opened = jnp.repeat(jnp.repeat(lay_sub > 0, BLK, axis=0), BLK, axis=1)
    pos_q = q_start + lax.broadcasted_iota(jnp.int32, (rows, cols), 0)
    pos_k = k_start + lax.broadcasted_iota(jnp.int32, (rows, cols), 1)
    allowed = opened & (pos_k <= pos_q)
    return (scores, allowed)


def layout_sub(lay, q_tile, k_tile, per_tile):
    return lax.dynamic_slice(lay, (q_tile * per_tile, k_tile * per_tile), (per_tile, per_tile))


def forward_head(q, k, v, lay, lsc, tile):
    length, width = q.shape
    steps = length // tile
    per_tile = tile // BLK
    scale = jnp.exp(lsc) / math.sqrt(HD)

    def forward_query_step(qt, carry):
        out_all, top_all, total_all = carry
        q_start = qt * tile
        q_rows = lax.dynamic_slice_in_dim(q, q_start, tile, 0)

        def stats_step(kt, state):
            sub = layout_sub(lay, qt, kt, per_tile)

            def stats_work(inner):
                top, total = inner
                k_tile = lax.dynamic_slice_in_dim(k, kt * tile, tile, 0)
                scores, allowed = tile_scores(q_rows, k_tile, sub, q_start, kt * tile, scale)
                masked = jnp.where(allowed, scores, BIG_NEG)
                newtop = jnp.maximum(top, jnp.max(masked, axis=1))
                total = total * jnp.exp(top - newtop) + jnp.sum(
                    jnp.exp(masked - newtop[:, None]), axis=1
                )
                return (newtop, total)

            return lax.cond(jnp.any(sub > 0), stats_work, lambda inner: inner, state)

        top, total = lax.fori_loop(
            0,
            qt + 1,
            stats_step,
            (jnp.full((tile,), BIG_NEG, jnp.float32), jnp.zeros((tile,), jnp.float32)),
        )

        def value_step(kt, acc):
            sub = layout_sub(lay, qt, kt, per_tile)

            def value_work(inner):
                k_tile = lax.dynamic_slice_in_dim(k, kt * tile, tile, 0)
                v_tile = lax.dynamic_slice_in_dim(v, kt * tile, tile, 0)
                scores, allowed = tile_scores(q_rows, k_tile, sub, q_start, kt * tile, scale)
                masked = jnp.where(allowed, scores, BIG_NEG)
                probs = jnp.exp(masked - top[:, None]) / total[:, None]
                return inner + jnp.dot(
                    probs.astype(jnp.bfloat16), v_tile, preferred_element_type=jnp.float32
                )

            return lax.cond(jnp.any(sub > 0), value_work, lambda inner: inner, acc)

        o_rows = lax.fori_loop(0, qt + 1, value_step, jnp.zeros((tile, width), jnp.float32)).astype(
            jnp.bfloat16
        )
        out_all = lax.dynamic_update_slice_in_dim(out_all, o_rows, q_start, 0)
        top_all = lax.dynamic_update_slice_in_dim(top_all, top, q_start, 0)
        total_all = lax.dynamic_update_slice_in_dim(total_all, total, q_start, 0)
        return (out_all, top_all, total_all)

    init = (
        jnp.zeros((length, width), jnp.bfloat16),
        jnp.zeros((length,), jnp.float32),
        jnp.zeros((length,), jnp.float32),
    )
    return lax.fori_loop(0, steps, forward_query_step, init)


def backward_head(q, k, v, g, out_all, top_all, total_all, lay, lsc, tile):
    length, width = q.shape
    steps = length // tile
    per_tile = tile // BLK
    scale = jnp.exp(lsc) / math.sqrt(HD)

    def backward_query_step(qt, carry):
        dq_all, dk_acc, dv_acc, dls = carry
        q_start = qt * tile
        q_rows = lax.dynamic_slice_in_dim(q, q_start, tile, 0)
        g_rows = lax.dynamic_slice_in_dim(g, q_start, tile, 0)
        o_rows = lax.dynamic_slice_in_dim(out_all, q_start, tile, 0)
        top = lax.dynamic_slice_in_dim(top_all, q_start, tile, 0)
        total = lax.dynamic_slice_in_dim(total_all, q_start, tile, 0)
        delta = jnp.sum(g_rows.astype(jnp.float32) * o_rows.astype(jnp.float32), axis=1)

        def key_step(kt, state):
            sub = layout_sub(lay, qt, kt, per_tile)

            def key_work(inner):
                dq_rows, dk_inner, dv_inner, dls_inner = inner
                k_start = kt * tile
                k_tile = lax.dynamic_slice_in_dim(k, k_start, tile, 0)
                v_tile = lax.dynamic_slice_in_dim(v, k_start, tile, 0)
                scores, allowed = tile_scores(q_rows, k_tile, sub, q_start, k_start, scale)
                masked = jnp.where(allowed, scores, BIG_NEG)
                probs = jnp.exp(masked - top[:, None]) / total[:, None]
                probs_b = probs.astype(jnp.bfloat16)
                dprobs = jnp.einsum("qd,kd->qk", g_rows, v_tile, preferred_element_type=jnp.float32)
                dscores = probs * (dprobs - delta[:, None])
                dls_inner = dls_inner + jnp.sum(jnp.where(allowed, dscores * scores, 0.0))
                dscores_b = (dscores * scale).astype(jnp.bfloat16)
                dq_rows = dq_rows + jnp.dot(dscores_b, k_tile, preferred_element_type=jnp.float32)
                dk_part = jnp.einsum(
                    "qk,qd->kd", dscores_b, q_rows, preferred_element_type=jnp.float32
                )
                dv_part = jnp.einsum(
                    "qk,qd->kd", probs_b, g_rows, preferred_element_type=jnp.float32
                )
                dk_inner = lax.dynamic_update_slice_in_dim(
                    dk_inner,
                    lax.dynamic_slice_in_dim(dk_inner, k_start, tile, 0) + dk_part,
                    k_start,
                    0,
                )
                dv_inner = lax.dynamic_update_slice_in_dim(
                    dv_inner,
                    lax.dynamic_slice_in_dim(dv_inner, k_start, tile, 0) + dv_part,
                    k_start,
                    0,
                )
                return (dq_rows, dk_inner, dv_inner, dls_inner)

            return lax.cond(jnp.any(sub > 0), key_work, lambda inner: inner, state)

        dq_rows, dk_acc, dv_acc, dls = lax.fori_loop(
            0, qt + 1, key_step, (jnp.zeros((tile, width), jnp.float32), dk_acc, dv_acc, dls)
        )
        dq_all = lax.dynamic_update_slice_in_dim(dq_all, dq_rows.astype(jnp.bfloat16), q_start, 0)
        return (dq_all, dk_acc, dv_acc, dls)

    init = (
        jnp.zeros((length, width), jnp.bfloat16),
        jnp.zeros((length, width), jnp.float32),
        jnp.zeros((length, width), jnp.float32),
        jnp.float32(0.0),
    )
    dq_all, dk_acc, dv_acc, dls = lax.fori_loop(0, steps, backward_query_step, init)
    return (dq_all, dk_acc.astype(jnp.bfloat16), dv_acc.astype(jnp.bfloat16), dls)


def body_by_heads(query, key, value, grad_out, layout, log_scale):
    tok_rows = query.shape[1]
    parts = lax.axis_size("seq")
    local = HEADS // parts
    first = lax.axis_index("seq") * local
    balanced = False
    head_of_slot = jnp.arange(HEADS, dtype=jnp.int32)
    my_heads = lax.dynamic_slice_in_dim(head_of_slot, first, local, 0)
    my_layout = jnp.take(layout, my_heads, axis=0)
    my_scale = jnp.take(log_scale, my_heads, axis=0)

    def by_heads(x):
        shaped = x.reshape(tok_rows, HEADS, HD)
        return shaped

    out_list, dq_list, dk_list, dv_list, dls_list = ([], [], [], [], [])
    q_heads, k_heads, v_heads, g_heads = (
        lax.all_to_all(by_heads(query), "seq", split_axis=1, concat_axis=0, tiled=True),
        lax.all_to_all(by_heads(key), "seq", split_axis=1, concat_axis=0, tiled=True),
        lax.all_to_all(by_heads(value), "seq", split_axis=1, concat_axis=0, tiled=True),
        lax.all_to_all(by_heads(grad_out), "seq", split_axis=1, concat_axis=0, tiled=True),
    )
    tile = min(512, q_heads.shape[0])
    for head in range(local):
        out_all, top_all, total_all = forward_head(
            q_heads[:, head],
            k_heads[:, head],
            v_heads[:, head],
            my_layout[head],
            my_scale[head],
            tile,
        )
        dq_all, dk_all, dv_all, dls = backward_head(
            q_heads[:, head],
            k_heads[:, head],
            v_heads[:, head],
            g_heads[:, head],
            out_all,
            top_all,
            total_all,
            my_layout[head],
            my_scale[head],
            tile,
        )
        out_list.append(out_all)
        dq_list.append(dq_all)
        dk_list.append(dk_all)
        dv_list.append(dv_all)
        dls_list.append(dls)
    stacked = (
        jnp.stack(out_list, axis=1),
        jnp.stack(dq_list, axis=1),
        jnp.stack(dk_list, axis=1),
        jnp.stack(dv_list, axis=1),
    )
    attended, grad_query, grad_key, grad_value = (
        lax.all_to_all(stacked[0], "seq", split_axis=0, concat_axis=1, tiled=True),
        lax.all_to_all(stacked[1], "seq", split_axis=0, concat_axis=1, tiled=True),
        lax.all_to_all(stacked[2], "seq", split_axis=0, concat_axis=1, tiled=True),
        lax.all_to_all(stacked[3], "seq", split_axis=0, concat_axis=1, tiled=True),
    )
    onehot = (my_heads[:, None] == jnp.arange(HEADS, dtype=jnp.int32)[None, :]).astype(jnp.float32)
    partial_grads = jnp.sum(jnp.stack(dls_list)[:, None] * onehot, axis=0)
    grad_log_scale = lax.psum(partial_grads, ("seq", "dp"))

    def flat(x):
        return x.reshape(1, tok_rows, HEADS * HD)

    return (flat(attended), flat(grad_query), flat(grad_key), flat(grad_value), grad_log_scale)


MESH = pl.DeviceIdType.MESH
GROUP = 2
LAG = 3
NT = (((1,), (1,)), ((), ()))
TN = (((0,), (0,)), ((), ()))
NN = (((1,), (0,)), ((), ()))


def mm(a, b, dims):
    return lax.dot_general(a, b, dims, preferred_element_type=jnp.float32)


def attend(q, k, v, g, mask, lsc):
    scale = jnp.exp(jnp.full((1, q.shape[0]), lsc, jnp.float32)) * (1.0 / math.sqrt(HD))
    scores = mm(k, q, NT) * scale
    masked = mask(scores)
    top = jnp.max(masked, axis=0, keepdims=True)
    expo = jnp.exp(masked - top)
    probs = expo * (1.0 / jnp.sum(expo, axis=0, keepdims=True))
    probs_b = probs.astype(jnp.bfloat16)
    out = mm(probs_b, v, TN)
    dprobs = mm(v, g, NT)
    weighed = probs * dprobs
    delta = jnp.sum(weighed, axis=0, keepdims=True)
    dscores = weighed - probs * delta
    dls = jnp.sum(dscores * scores, axis=0, keepdims=True)
    dscores_b = (dscores * scale).astype(jnp.bfloat16)
    dq = mm(dscores_b, k, TN)
    dk = mm(dscores_b, q, NN)
    dv = mm(probs_b, g, NN)
    return out, dq, dk, dv, dls


def line_kernel(
    heads, lay, lsc, q, k, v, g, o, dq, dk, dv, dls, rb, lb, rsrc, lsrc, acc, rsend, rrecv, lsend, lrecv
):
    me = lax.axis_index("seq")
    parts = 4
    right, left = lax.rem(me + 1, parts), lax.rem(me + parts - 1, parts)
    chunks = heads // GROUP
    width = GROUP * HD
    bf = jnp.bfloat16

    def cols(c):
        return pl.ds(pl.multiple_of(c * width, width), width)

    def head_cols(h):
        return pl.ds(pl.multiple_of(h * HD, HD), HD)

    def to_right(src, dst, kind, c):
        return pltpu.make_async_remote_copy(
            src_ref=src.at[:, cols(c)], dst_ref=dst.at[:, cols(c)],
            send_sem=rsend.at[kind, c], recv_sem=rrecv.at[kind, c],
            device_id={"seq": right}, device_id_type=MESH,
        )

    def to_left(src, dst, kind, c):
        return pltpu.make_async_remote_copy(
            src_ref=src.at[:, cols(c)], dst_ref=dst.at[:, cols(c)],
            send_sem=lsend.at[kind, c], recv_sem=lrecv.at[kind, c],
            device_id={"seq": left}, device_id_type=MESH,
        )

    def wait_right(kinds, c):
        for kind in range(kinds):
            to_right(rb.at[kind], rb.at[kind], kind, c).wait_recv()

    def wait_left(kinds, c):
        for kind in range(kinds):
            to_left(lb.at[kind], lb.at[kind], kind, c).wait_recv()

    def drain(rights, lefts):
        def step(c, carry):
            for kind in range(rights):
                to_right(rb.at[kind], rb.at[kind], kind, c).wait_send()
            for kind in range(lefts):
                to_left(lb.at[kind], lb.at[kind], kind, c).wait_send()
            return carry

        lax.fori_loop(0, chunks, step, 0)

    def closed(h, row, col):
        return (lay[(h * parts + row) * parts + col] - 1).astype(jnp.float32) * -BIG_NEG

    def blocks_mask(h, rows, scores):
        after = lax.broadcasted_iota(jnp.int32, (BLK, BLK), 0) > lax.broadcasted_iota(jnp.int32, (BLK, BLK), 1)
        bands = []
        for col in range(scores.shape[0] // BLK):
            line = []
            for at, row in enumerate(rows):
                block = scores[col * BLK : (col + 1) * BLK, at * BLK : (at + 1) * BLK]
                if col > row:
                    block = jnp.full((BLK, BLK), BIG_NEG, jnp.float32)
                elif col == row:
                    block = jnp.where(after, BIG_NEG, block)
                else:
                    block = block + closed(h, row, col)
                line.append(block)
            bands.append(line[0] if len(line) == 1 else jnp.concatenate(line, axis=1))
        return bands[0] if len(bands) == 1 else jnp.concatenate(bands, axis=0)

    def work(h, rows, qs, ks, vs, gs):
        def rows_of(refs):
            got = [r[:, head_cols(h)] for r in refs]
            return got[0] if len(got) == 1 else jnp.concatenate(got, axis=0)

        out = attend(
            rows_of(qs), rows_of(ks), rows_of(vs), rows_of(gs), functools.partial(blocks_mask, h, rows), lsc[h]
        )
        part = out[4][:, :HD]
        for at in range(1, len(rows)):
            part = part + out[4][:, at * HD : (at + 1) * HD]
        dls[pl.ds(h, 1), :] = part
        return out[:4]

    def block(x, at):
        return x[at * BLK : (at + 1) * BLK]

    barrier = pltpu.get_barrier_semaphore()

    @pl.when(me > 0)
    def _():
        pl.semaphore_signal(barrier, inc=1, device_id={"seq": left}, device_id_type=MESH)

    @pl.when(me < parts - 1)
    def _():
        pl.semaphore_signal(barrier, inc=1, device_id={"seq": right}, device_id_type=MESH)

    inside = (me > 0) & (me < parts - 1)

    @pl.when(inside)
    def _():
        pl.semaphore_wait(barrier, 2)

    @pl.when(jnp.logical_not(inside))
    def _():
        pl.semaphore_wait(barrier, 1)

    @pl.when(me == 0)
    def _():
        def send(c, carry):
            to_right(k, rb.at[0], 0, c).start()
            to_right(v, rb.at[1], 1, c).start()
            return carry

        lax.fori_loop(0, chunks, send, 0)

        def compute(c, carry):
            for i in range(GROUP):
                h = c * GROUP + i
                hc = head_cols(h)
                out, gq, gk, gv = work(h, (0,), (q,), (k,), (v,), (g,))
                o[:, hc] = out.astype(bf)
                dq[:, hc] = gq.astype(bf)
                acc[0, :, hc] = gk
                acc[1, :, hc] = gv
            return carry

        lax.fori_loop(0, chunks, compute, 0)

        def finish(c, carry):
            wait_left(2, c)
            cc = cols(c)
            dk[:, cc] = (acc[0, :, cc] + lb[0, :, cc].astype(jnp.float32)).astype(bf)
            dv[:, cc] = (acc[1, :, cc] + lb[1, :, cc].astype(jnp.float32)).astype(bf)
            return carry

        lax.fori_loop(0, chunks, finish, 0)
        drain(2, 0)

    @pl.when(me == 1)
    def _():
        def finish(c):
            wait_left(4, c)
            cc = cols(c)
            for kind in range(2):
                lsrc[kind, :, cc] = (acc[kind, :, cc] + lb[kind, :, cc].astype(jnp.float32)).astype(bf)
                to_left(lsrc.at[kind], lb.at[kind], kind, c).start()
            dk[:, cc] = (acc[2, :, cc] + lb[2, :, cc].astype(jnp.float32)).astype(bf)
            dv[:, cc] = (acc[3, :, cc] + lb[3, :, cc].astype(jnp.float32)).astype(bf)

        def step(c, carry):
            to_right(k, rb.at[2], 2, c).start()
            to_right(v, rb.at[3], 3, c).start()
            wait_right(2, c)
            to_right(rb.at[0], rb.at[0], 0, c).start()
            to_right(rb.at[1], rb.at[1], 1, c).start()
            for i in range(GROUP):
                h = c * GROUP + i
                hc = head_cols(h)
                out, gq, gk, gv = work(h, (1,), (q,), (rb.at[0], k), (rb.at[1], v), (g,))
                o[:, hc] = out.astype(bf)
                dq[:, hc] = gq.astype(bf)
                acc[0, :, hc] = block(gk, 0)
                acc[1, :, hc] = block(gv, 0)
                acc[2, :, hc] = block(gk, 1)
                acc[3, :, hc] = block(gv, 1)

            @pl.when(c >= LAG)
            def _():
                finish(c - LAG)

            return carry

        lax.fori_loop(0, chunks, step, 0)

        def tail(c, carry):
            finish(c)
            return carry

        lax.fori_loop(max(chunks - LAG, 0), chunks, tail, 0)
        drain(4, 2)

    @pl.when(me == 2)
    def _():
        def step(c, carry):
            wait_left(4, c)
            wait_right(4, c)
            for i in range(GROUP):
                h = c * GROUP + i
                hc = head_cols(h)
                out, gq, gk, gv = work(
                    h, (2, 3), (q, lb.at[0]), (rb.at[0], rb.at[2], k, lb.at[1]),
                    (rb.at[1], rb.at[3], v, lb.at[2]), (g, lb.at[3]),
                )
                o[:, hc] = block(out, 0).astype(bf)
                dq[:, hc] = block(gq, 0).astype(bf)
                dk[:, hc] = block(gk, 2).astype(bf)
                dv[:, hc] = block(gv, 2).astype(bf)
                rsrc[0, :, hc] = block(out, 1).astype(bf)
                rsrc[1, :, hc] = block(gq, 1).astype(bf)
                rsrc[2, :, hc] = block(gk, 3).astype(bf)
                rsrc[3, :, hc] = block(gv, 3).astype(bf)
                lsrc[0, :, hc] = block(gk, 0).astype(bf)
                lsrc[1, :, hc] = block(gv, 0).astype(bf)
                lsrc[2, :, hc] = block(gk, 1).astype(bf)
                lsrc[3, :, hc] = block(gv, 1).astype(bf)
            for kind in range(4):
                to_left(lsrc.at[kind], lb.at[kind], kind, c).start()
            for kind, dst in enumerate((o, dq, dk, dv)):
                to_right(rsrc.at[kind], dst, kind, c).start()
            return carry

        lax.fori_loop(0, chunks, step, 0)
        drain(4, 4)

    @pl.when(me == 3)
    def _():
        def send(c, carry):
            for kind, src in enumerate((q, k, v, g)):
                to_left(src, lb.at[kind], kind, c).start()
            return carry

        lax.fori_loop(0, chunks, send, 0)
        dls[...] = jnp.zeros_like(dls)

        def collect(c, carry):
            for kind, dst in enumerate((o, dq, dk, dv)):
                to_right(dst, dst, kind, c).wait_recv()
            return carry

        lax.fori_loop(0, chunks, collect, 0)
        drain(0, 4)


def body(query, key, value, grad_out, layout, log_scale):
    _, rows, features = query.shape
    heads = features // HD
    if lax.axis_size("seq") != 4 or rows != BLK or query.shape[0] != 1:
        return body_by_heads(query, key, value, grad_out, layout, log_scale)
    flat = jax.ShapeDtypeStruct((rows, features), jnp.bfloat16)
    chunks = heads // GROUP
    vmem = pl.BlockSpec(memory_space=pltpu.VMEM)
    smem = pl.BlockSpec(memory_space=pltpu.SMEM)
    landing = pltpu.VMEM((4, rows, features), jnp.bfloat16)
    sems = pltpu.SemaphoreType.DMA((4, chunks))
    out, dq, dk, dv, dls = pl.pallas_call(
        functools.partial(line_kernel, heads),
        out_shape=(flat, flat, flat, flat, jax.ShapeDtypeStruct((heads, HD), jnp.float32)),
        in_specs=[smem, smem, vmem, vmem, vmem, vmem],
        out_specs=[vmem] * 5,
        scratch_shapes=[landing] * 4
        + [pltpu.VMEM((4, rows, features), jnp.float32)]
        + [sems] * 4,
        compiler_params=pltpu.CompilerParams(
            collective_id=0, has_side_effects=True, vmem_limit_bytes=48 * 1024 * 1024
        ),
    )(
        layout.reshape(-1),
        log_scale,
        *(x.reshape(rows, features) for x in (query, key, value, grad_out)),
    )
    grad_log_scale = lax.psum(jnp.sum(dls, axis=1), ("seq", "dp"))
    return tuple(x.reshape(1, rows, features) for x in (out, dq, dk, dv)) + (grad_log_scale,)


def solution(mesh):
    return jax.shard_map(
        body,
        mesh=mesh,
        in_specs=(
            P(("groups", "dp"), "seq", None),
            P(("groups", "dp"), "seq", None),
            P(("groups", "dp"), "seq", None),
            P(("groups", "dp"), "seq", None),
            P(),
            P(),
        ),
        out_specs=(
            P(("groups", "dp"), "seq", None),
            P(("groups", "dp"), "seq", None),
            P(("groups", "dp"), "seq", None),
            P(("groups", "dp"), "seq", None),
            P("groups"),
        ),
        check_vma=False,
    )
```

profile of v0, /device:TPU:0, one launch (start us, length us, event | category | flops | bytes accessed | tf_op | source)
XLA Modules:
  0.0 153.3 jit_solution(18173713329743640026)
XLA Ops:
  0.6 0.8 copy.11
  1.4 0.0 copy-start.2
  1.4 0.1 reshape.37.lay
  1.6 0.5 copy-done.2
  2.1 0.0 copy-start.1
  2.1 1.2 copy-done.1
  3.3 113.7 %shard_map.101 = (bf16[128,4096]{1,0:T(8,128)(2,1)S(1)}, bf16[128,4096]{1,0:T(8,128)(2,1)S(1)}, bf16[128,4096]{1,0:T(8,128)(2,1)S(1)}, bf16[128,4096]{1,0:T(8,128)(2,1)S(1)}, f32[32,128]{1,0:T(8,128)S(1)}) custom-call(s32[512]{0:T(512)S(1)} %reshape.37.lay, f32[32]{0:T(128)S(1)} %copy-done.2, bf16[128,4096]{1,0:T(8,128)(2,1)S(1)} %bitcast.12, ...), custom_call_target="tpu_custom_call" | custom-call | tf_op jit(solution)/shard_map/pallas_call | solution.py:517
  117.0 0.0 copy-start
  117.1 1.0 copy-done
  118.0 0.1 reduce_sum.9
  118.1 30.0 %psum.7 = f32[32]{0:T(128)} all-reduce(f32[32]{0:T(128)S(1)} %reduce_sum.9), channel_id=1, replica_groups=mesh['groups'=2,'seq'=4,'dp'=4] {'seq','dp'}, use_global_device_ids=true, to_apply=%region_1.0 | all-reduce | flops 32 | bytes 256 | tf_op jit(solution)/shard_map/psum | solution.py:533
  148.1 2.3 %copy.16 = bf16[1,128,4096]{2,1,0:T(8,128)(2,1)} copy(bf16[1,128,4096]{2,1,0:T(8,128)(2,1)} %bitcast.11) | data formatting | bytes 2097152
  150.4 1.0 copy.17
  151.4 1.0 copy.18
  152.4 1.0 copy.19
Async XLA Ops:
  1.4 0.7 copy-start.2
  2.1 1.2 copy-start.1
  117.0 1.0 copy-start
where the time goes:
time: 154 us; the launch traced here: 153 us
  Pallas kernels  114 us (74%)
  blocking collectives  30 us (19%)
  local copies, waits for them, and re-layouts  8.84 us (6%)
    pallas_call x1, Pallas kernels, body(): pl.pallas_call(functools.partial(line_kernel, heads), out_shape=(flat, fl...  114 us
    psum x1, blocking collectives, body(): grad_log_scale = lax.psum(jnp.sum(dls, axis=1), ('seq', 'dp'))  30 us
    unnamed x11, local copies, waits for them, and re-layouts  8.72 us

commit v1 on v0

--- a/solution.py
+++ b/solution.py
@@ -239,8 +239,9 @@
 
 
 MESH = pl.DeviceIdType.MESH
-GROUP = 2
-LAG = 3
+GROUP = 1
+LAG = 10
+AHEAD = 3
 NT = (((1,), (1,)), ((), ()))
 TN = (((0,), (0,)), ((), ()))
 NN = (((1,), (0,)), ((), ()))
@@ -272,14 +273,18 @@
 
 
 def line_kernel(
-    heads, lay, lsc, q, k, v, g, o, dq, dk, dv, dls, rb, lb, rsrc, lsrc, acc, rsend, rrecv, lsend, lrecv
+    heads, dps, lay, lsc, q, k, v, g, o, dq, dk, dv, dls,
+    own, rb, lb, rsrc, lsrc, acc, dloc, dgot, rsend, rrecv, lsend, lrecv, dsend, drecv, isem
 ):
     me = lax.axis_index("seq")
+    at_dp = lax.axis_index("dp")
     parts = 4
     right, left = lax.rem(me + 1, parts), lax.rem(me + parts - 1, parts)
     chunks = heads // GROUP
     width = GROUP * HD
     bf = jnp.bfloat16
+    outs = (o, dq, dk, dv)
+    first, second = pl.ds(0, 2), pl.ds(2, 2)
 
     def cols(c):
         return pl.ds(pl.multiple_of(c * width, width), width)
@@ -287,40 +292,57 @@
     def head_cols(h):
         return pl.ds(pl.multiple_of(h * HD, HD), HD)
 
-    def to_right(src, dst, kind, c):
+    def to_right(src, dst, pair, c):
         return pltpu.make_async_remote_copy(
-            src_ref=src.at[:, cols(c)], dst_ref=dst.at[:, cols(c)],
-            send_sem=rsend.at[kind, c], recv_sem=rrecv.at[kind, c],
+            src_ref=src, dst_ref=dst, send_sem=rsend.at[pair, c], recv_sem=rrecv.at[pair, c],
             device_id={"seq": right}, device_id_type=MESH,
         )
 
-    def to_left(src, dst, kind, c):
+    def to_left(src, dst, pair, c):
         return pltpu.make_async_remote_copy(
-            src_ref=src.at[:, cols(c)], dst_ref=dst.at[:, cols(c)],
-            send_sem=lsend.at[kind, c], recv_sem=lrecv.at[kind, c],
+            src_ref=src, dst_ref=dst, send_sem=lsend.at[pair, c], recv_sem=lrecv.at[pair, c],
             device_id={"seq": left}, device_id_type=MESH,
         )
 
-    def wait_right(kinds, c):
-        for kind in range(kinds):
-            to_right(rb.at[kind], rb.at[kind], kind, c).wait_recv()
-
-    def wait_left(kinds, c):
-        for kind in range(kinds):
-            to_left(lb.at[kind], lb.at[kind], kind, c).wait_recv()
+    def both(buf, pair, c):
+        return buf.at[second if pair else first, :, cols(c)]
+
+    def wait_right(pairs, c):
+        for pair in range(pairs):
+            to_right(both(rb, pair, c), both(rb, pair, c), pair, c).wait_recv()
+
+    def wait_left(pairs, c):
+        for pair in range(pairs):
+            to_left(both(lb, pair, c), both(lb, pair, c), pair, c).wait_recv()
 
     def drain(rights, lefts):
         def step(c, carry):
-            for kind in range(rights):
-                to_right(rb.at[kind], rb.at[kind], kind, c).wait_send()
-            for kind in range(lefts):
-                to_left(lb.at[kind], lb.at[kind], kind, c).wait_send()
+            for pair in range(rights):
+                to_right(both(rb, pair, c), both(rb, pair, c), pair, c).wait_send()
+            for pair in range(lefts):
+                to_left(both(lb, pair, c), both(lb, pair, c), pair, c).wait_send()
             return carry
 
         lax.fori_loop(0, chunks, step, 0)
 
+    def move(src, dst, send, recv, **device):
+        return pltpu.make_async_remote_copy(
+            src_ref=src, dst_ref=dst, send_sem=dsend.at[send], recv_sem=drecv.at[recv],
+            device_id=device, device_id_type=MESH,
+        )
+
+    def total_out():
+        move(dloc, dls, 0, 2, seq=2).wait_recv()
+
+    load = [pltpu.make_async_copy(x, own.at[at], isem.at[at]) for at, x in enumerate((q, k, v, g))]
+    oq, ok, ov, og = (own.at[at] for at in range(4))
+
+    def loaded():
+        for copy in load:
+            copy.wait()
+
     def closed(h, row, col):
-        return (lay[(h * parts + row) * parts + col] - 1).astype(jnp.float32) * -BIG_NEG
+        return (lay[row, col, h] - 1).astype(jnp.float32) * -BIG_NEG
 
     def blocks_mask(h, rows, scores):
         after = lax.broadcasted_iota(jnp.int32, (BLK, BLK), 0) > lax.broadcasted_iota(jnp.int32, (BLK, BLK), 1)
@@ -350,46 +372,63 @@
         part = out[4][:, :HD]
         for at in range(1, len(rows)):
             part = part + out[4][:, at * HD : (at + 1) * HD]
-        dls[pl.ds(h, 1), :] = part
+        dloc[pl.ds(h, 1), :] = part
         return out[:4]
 
     def block(x, at):
         return x[at * BLK : (at + 1) * BLK]
 
+    @pl.when(me < 3)
+    def _():
+        for copy in load:
+            copy.start()
+
     barrier = pltpu.get_barrier_semaphore()
 
-    @pl.when(me > 0)
-    def _():
-        pl.semaphore_signal(barrier, inc=1, device_id={"seq": left}, device_id_type=MESH)
-
-    @pl.when(me < parts - 1)
-    def _():
-        pl.semaphore_signal(barrier, inc=1, device_id={"seq": right}, device_id_type=MESH)
-
-    inside = (me > 0) & (me < parts - 1)
-
-    @pl.when(inside)
-    def _():
+    def greet(**device):
+        pl.semaphore_signal(barrier, inc=1, device_id=device, device_id_type=MESH)
+
+    @pl.when(me == 0)
+    def _():
+        greet(seq=1)
+        greet(seq=2)
         pl.semaphore_wait(barrier, 2)
 
-    @pl.when(jnp.logical_not(inside))
-    def _():
+    @pl.when(me == 1)
+    def _():
+        greet(seq=0)
+        greet(seq=2)
+        pl.semaphore_wait(barrier, 2)
+
+    @pl.when(me == 2)
+    def _():
+        greet(seq=0)
+        greet(seq=1)
+        greet(seq=3)
+        for step in range(1, dps):
+            greet(dp=lax.rem(at_dp + step, dps))
+        pl.semaphore_wait(barrier, 3 + dps - 1)
+
+    @pl.when(me == 3)
+    def _():
+        greet(seq=2)
         pl.semaphore_wait(barrier, 1)
 
     @pl.when(me == 0)
     def _():
         def send(c, carry):
-            to_right(k, rb.at[0], 0, c).start()
-            to_right(v, rb.at[1], 1, c).start()
+            to_right(k.at[:, cols(c)], rb.at[0, :, cols(c)], 0, c).start()
+            to_right(v.at[:, cols(c)], rb.at[1, :, cols(c)], 0, c).start()
             return carry
 
         lax.fori_loop(0, chunks, send, 0)
+        loaded()
 
         def compute(c, carry):
             for i in range(GROUP):
                 h = c * GROUP + i
                 hc = head_cols(h)
-                out, gq, gk, gv = work(h, (0,), (q,), (k,), (v,), (g,))
+                out, gq, gk, gv = work(h, (0,), (oq,), (ok,), (ov,), (og,))
                 o[:, hc] = out.astype(bf)
                 dq[:, hc] = gq.astype(bf)
                 acc[0, :, hc] = gk
@@ -397,38 +436,53 @@
             return carry
 
         lax.fori_loop(0, chunks, compute, 0)
+        mine = move(dloc, dgot.at[0], 0, 0, seq=2)
+        mine.start()
 
         def finish(c, carry):
-            wait_left(2, c)
+            wait_left(1, c)
             cc = cols(c)
             dk[:, cc] = (acc[0, :, cc] + lb[0, :, cc].astype(jnp.float32)).astype(bf)
             dv[:, cc] = (acc[1, :, cc] + lb[1, :, cc].astype(jnp.float32)).astype(bf)
             return carry
 
         lax.fori_loop(0, chunks, finish, 0)
-        drain(2, 0)
+        drain(1, 0)
+        mine.wait_send()
+        total_out()
 
     @pl.when(me == 1)
     def _():
+        def send_own(c):
+            to_right(k.at[:, cols(c)], rb.at[2, :, cols(c)], 1, c).start()
+            to_right(v.at[:, cols(c)], rb.at[3, :, cols(c)], 1, c).start()
+
         def finish(c):
-            wait_left(4, c)
+            wait_left(2, c)
             cc = cols(c)
             for kind in range(2):
                 lsrc[kind, :, cc] = (acc[kind, :, cc] + lb[kind, :, cc].astype(jnp.float32)).astype(bf)
-                to_left(lsrc.at[kind], lb.at[kind], kind, c).start()
+            to_left(both(lsrc, 0, c), both(lb, 0, c), 0, c).start()
             dk[:, cc] = (acc[2, :, cc] + lb[2, :, cc].astype(jnp.float32)).astype(bf)
             dv[:, cc] = (acc[3, :, cc] + lb[3, :, cc].astype(jnp.float32)).astype(bf)
 
+        ahead = min(AHEAD, chunks)
+        for c in range(ahead):
+            send_own(c)
+        loaded()
+
         def step(c, carry):
-            to_right(k, rb.at[2], 2, c).start()
-            to_right(v, rb.at[3], 3, c).start()
-            wait_right(2, c)
-            to_right(rb.at[0], rb.at[0], 0, c).start()
-            to_right(rb.at[1], rb.at[1], 1, c).start()
+            wait_right(1, c)
+            to_right(both(rb, 0, c), both(rb, 0, c), 0, c).start()
+
+            @pl.when(c + ahead < chunks)
+            def _():
+                send_own(c + ahead)
+
             for i in range(GROUP):
                 h = c * GROUP + i
                 hc = head_cols(h)
-                out, gq, gk, gv = work(h, (1,), (q,), (rb.at[0], k), (rb.at[1], v), (g,))
+                out, gq, gk, gv = work(h, (1,), (oq,), (rb.at[0], ok), (rb.at[1], ov), (og,))
                 o[:, hc] = out.astype(bf)
                 dq[:, hc] = gq.astype(bf)
                 acc[0, :, hc] = block(gk, 0)
@@ -443,64 +497,99 @@
             return carry
 
         lax.fori_loop(0, chunks, step, 0)
+        mine = move(dloc, dgot.at[1], 0, 1, seq=2)
+        mine.start()
 
         def tail(c, carry):
             finish(c)
             return carry
 
         lax.fori_loop(max(chunks - LAG, 0), chunks, tail, 0)
-        drain(4, 2)
+        drain(2, 1)
+        mine.wait_send()
+        total_out()
 
     @pl.when(me == 2)
     def _():
+        loaded()
+
         def step(c, carry):
-            wait_left(4, c)
-            wait_right(4, c)
+            wait_left(2, c)
+            wait_right(2, c)
             for i in range(GROUP):
                 h = c * GROUP + i
                 hc = head_cols(h)
                 out, gq, gk, gv = work(
-                    h, (2, 3), (q, lb.at[0]), (rb.at[0], rb.at[2], k, lb.at[1]),
-                    (rb.at[1], rb.at[3], v, lb.at[2]), (g, lb.at[3]),
+                    h, (2, 3), (oq, lb.at[0]), (rb.at[0], rb.at[2], ok, lb.at[1]),
+                    (rb.at[1], rb.at[3], ov, lb.at[2]), (og, lb.at[3]),
                 )
+                lsrc[0, :, hc] = block(gk, 0).astype(bf)
+                lsrc[1, :, hc] = block(gv, 0).astype(bf)
+                lsrc[2, :, hc] = block(gk, 1).astype(bf)
+                lsrc[3, :, hc] = block(gv, 1).astype(bf)
+                rsrc[0, :, hc] = block(out, 1).astype(bf)
+                rsrc[1, :, hc] = block(gq, 1).astype(bf)
+                rsrc[2, :, hc] = block(gk, 3).astype(bf)
+                rsrc[3, :, hc] = block(gv, 3).astype(bf)
                 o[:, hc] = block(out, 0).astype(bf)
                 dq[:, hc] = block(gq, 0).astype(bf)
                 dk[:, hc] = block(gk, 2).astype(bf)
                 dv[:, hc] = block(gv, 2).astype(bf)
-                rsrc[0, :, hc] = block(out, 1).astype(bf)
-                rsrc[1, :, hc] = block(gq, 1).astype(bf)
-                rsrc[2, :, hc] = block(gk, 3).astype(bf)
-                rsrc[3, :, hc] = block(gv, 3).astype(bf)
-                lsrc[0, :, hc] = block(gk, 0).astype(bf)
-                lsrc[1, :, hc] = block(gv, 0).astype(bf)
-                lsrc[2, :, hc] = block(gk, 1).astype(bf)
-                lsrc[3, :, hc] = block(gv, 1).astype(bf)
-            for kind in range(4):
-                to_left(lsrc.at[kind], lb.at[kind], kind, c).start()
-            for kind, dst in enumerate((o, dq, dk, dv)):
-                to_right(rsrc.at[kind], dst, kind, c).start()
+            for pair in range(2):
+                to_left(both(lsrc, pair, c), both(lb, pair, c), pair, c).start()
+            for kind, dst in enumerate(outs):
+                to_right(rsrc.at[kind, :, cols(c)], dst.at[:, cols(c)], kind // 2, c).start()
             return carry
 
         lax.fori_loop(0, chunks, step, 0)
-        drain(4, 4)
+        for part in range(2):
+            move(dloc, dgot.at[part], 0, part, seq=part).wait_recv()
+        dgot[2 + at_dp] = dloc[...] + dgot[0] + dgot[1]
+        crossing = [
+            move(dgot.at[2 + at_dp], dgot.at[2 + at_dp], step, 2 + step, dp=lax.rem(at_dp + step, dps))
+            for step in range(1, dps)
+        ]
+        for copy in crossing:
+            copy.start()
+        for copy in crossing:
+            copy.wait_recv()
+        total = dgot[2]
+        for part in range(1, dps):
+            total = total + dgot[2 + part]
+        dls[...] = total
+        back = [move(dls, dls, dps + at, 2, seq=part) for at, part in enumerate((0, 1, 3))]
+        for copy in back:
+            copy.start()
+        drain(2, 2)
+        for copy in crossing + back:
+            copy.wait_send()
 
     @pl.when(me == 3)
     def _():
         def send(c, carry):
             for kind, src in enumerate((q, k, v, g)):
-                to_left(src, lb.at[kind], kind, c).start()
+                to_left(src.at[:, cols(c)], lb.at[kind, :, cols(c)], kind // 2, c).start()
             return carry
 
         lax.fori_loop(0, chunks, send, 0)
-        dls[...] = jnp.zeros_like(dls)
 
         def collect(c, carry):
-            for kind, dst in enumerate((o, dq, dk, dv)):
-                to_right(dst, dst, kind, c).wait_recv()
+            wait_right(2, c)
             return carry
 
         lax.fori_loop(0, chunks, collect, 0)
-        drain(0, 4)
+        drain(0, 2)
+        total_out()
+
+
+def write_kernel(*refs):
+    count = len(refs) // 2
+    sems = refs[-1]
+    copies = [pltpu.make_async_copy(refs[at], refs[count + at], sems.at[at]) for at in range(count)]
+    for copy in copies:
+        copy.start()
+    for copy in copies:
+        copy.wait()
 
 
 def body(query, key, value, grad_out, layout, log_scale):
@@ -508,30 +597,48 @@
     heads = features // HD
     if lax.axis_size("seq") != 4 or rows != BLK or query.shape[0] != 1:
         return body_by_heads(query, key, value, grad_out, layout, log_scale)
+    dps = lax.axis_size("dp")
     flat = jax.ShapeDtypeStruct((rows, features), jnp.bfloat16)
     chunks = heads // GROUP
     vmem = pl.BlockSpec(memory_space=pltpu.VMEM)
     smem = pl.BlockSpec(memory_space=pltpu.SMEM)
+    hbm = pl.BlockSpec(memory_space=pltpu.HBM)
     landing = pltpu.VMEM((4, rows, features), jnp.bfloat16)
-    sems = pltpu.SemaphoreType.DMA((4, chunks))
-    out, dq, dk, dv, dls = pl.pallas_call(
-        functools.partial(line_kernel, heads),
+    sems = pltpu.SemaphoreType.DMA((2, chunks))
+    *results, dls = pl.pallas_call(
+        functools.partial(line_kernel, heads, dps),
         out_shape=(flat, flat, flat, flat, jax.ShapeDtypeStruct((heads, HD), jnp.float32)),
-        in_specs=[smem, smem, vmem, vmem, vmem, vmem],
+        in_specs=[smem, smem, hbm, hbm, hbm, hbm],
         out_specs=[vmem] * 5,
-        scratch_shapes=[landing] * 4
-        + [pltpu.VMEM((4, rows, features), jnp.float32)]
-        + [sems] * 4,
+        scratch_shapes=[landing] * 5
+        + [
+            pltpu.VMEM((4, rows, features), jnp.float32),
+            pltpu.VMEM((heads, HD), jnp.float32),
+            pltpu.VMEM((2 + dps, heads, HD), jnp.float32),
+        ]
+        + [sems] * 4
+        + [
+            pltpu.SemaphoreType.DMA((dps + 3,)),
+            pltpu.SemaphoreType.DMA((dps + 2,)),
+            pltpu.SemaphoreType.DMA((4,)),
+        ],
         compiler_params=pltpu.CompilerParams(
             collective_id=0, has_side_effects=True, vmem_limit_bytes=48 * 1024 * 1024
         ),
     )(
-        layout.reshape(-1),
+        layout.transpose(1, 2, 0),
         log_scale,
         *(x.reshape(rows, features) for x in (query, key, value, grad_out)),
     )
-    grad_log_scale = lax.psum(jnp.sum(dls, axis=1), ("seq", "dp"))
-    return tuple(x.reshape(1, rows, features) for x in (out, dq, dk, dv)) + (grad_log_scale,)
+    results = pl.pallas_call(
+        write_kernel,
+        out_shape=(flat, flat, flat, flat),
+        in_specs=[vmem] * 4,
+        out_specs=[hbm] * 4,
+        scratch_shapes=[pltpu.SemaphoreType.DMA((4,))],
+        compiler_params=pltpu.CompilerParams(vmem_limit_bytes=16 * 1024 * 1024),
+    )(*results)
+    return tuple(x.reshape(1, rows, features) for x in results) + (jnp.sum(dls, axis=1),)
 
 
 def solution(mesh):

time: 154 us -> 117 us (0.76)
  blocking collectives: 30 us -> 0 us
  local copies, waits for them, and re-layouts: 8.84 us -> 1.91 us
    psum x1 -> x0, blocking collectives: 30 us -> none  [body(): grad_log_scale = lax.psum(jnp.sum(dls, axis=1), ('seq', 'dp'))]
    unnamed x11 -> x6, local copies, waits for them, and re-layouts: 8.72 us -> 1.91 us
    pallas_call x1 -> x2, Pallas kernels: 114 us -> 114 us  [the longest x1 112 us: body(): pl.pallas_call(functools.partial(line_kernel, heads, dps), out_shape=(fla...]
where the time goes in v1:
time: 117 us
  Pallas kernels  114 us (97%)
  local copies, waits for them, and re-layouts  1.91 us (2%)
    pallas_call x1, Pallas kernels, body(): pl.pallas_call(functools.partial(line_kernel, heads, dps), out_shape=(fla...  112 us

profile of v1, /device:TPU:0, one launch (start us, length us, event | category | flops | bytes accessed | tf_op | source)
XLA Modules:
  0.0 116.7 jit_solution(4679977616467390887)
XLA Ops:
  0.6 0.0 copy-start.1
  0.6 0.0 copy-start.2
  0.7 0.7 copy-done.1
  1.3 0.0 copy-done.2
  1.3 0.0 copy-start
  1.3 1.2 %copy-done = bf16[1,128,4096]{2,1,0:T(8,128)(2,1)S(1)} copy-done((bf16[1,128,4096]{2,1,0:T(8,128)(2,1)S(1)}, bf16[1,128,4096]{2,1,0:T(8,128)(2,1)}, u32[]{:S(2)}) %copy-start) | copy-done | bytes 1048600
  2.6 111.5 %shard_map.101 = (bf16[128,4096]{1,0:T(8,128)(2,1)S(1)}, bf16[128,4096]{1,0:T(8,128)(2,1)S(1)}, bf16[128,4096]{1,0:T(8,128)(2,1)S(1)}, bf16[128,4096]{1,0:T(8,128)(2,1)S(1)}, f32[32,128]{1,0:T(8,128)S(1)}) custom-call(s32[4,4,32]{2,1,0:T(4,128)S(1)} %bitcast.10, f32[32]{0:T(128)S(1)} %copy-done.2, bf16[128,4096]{1,0:T(8,128)(2,1)S(1)} %bitcast.9, ...), custom_call_target="tpu_custom_call" | custom-call | tf_op jit(solution)/shard_map/pallas_call | solution.py:608
  114.1 2.0 %shard_map.102 = (bf16[128,4096]{1,0:T(8,128)(2,1)}, bf16[128,4096]{1,0:T(8,128)(2,1)}, bf16[128,4096]{1,0:T(8,128)(2,1)}, bf16[128,4096]{1,0:T(8,128)(2,1)}) custom-call(bf16[128,4096]{1,0:T(8,128)(2,1)S(1)} %get-tuple-element.14.refs_0_, bf16[128,4096]{1,0:T(8,128)(2,1)S(1)} %get-tuple-element.15.refs_1_, bf16[128,4096]{1,0:T(8,128)(2,1)S(1)} %get-tuple-element.16.refs_2_, ...), custom_call_target="tpu_custom_call" | custom-call | tf_op jit(solution)/shard_map/pallas_call | solution.py:633
  116.1 0.6 reduce_sum.9
Async XLA Ops:
  0.6 0.7 copy-start.1
  0.6 0.7 copy-start.2
  1.3 1.2 %copy-start = (bf16[1,128,4096]{2,1,0:T(8,128)(2,1)S(1)}, bf16[1,128,4096]{2,1,0:T(8,128)(2,1)}, u32[]{:S(2)}) copy-start(bf16[1,128,4096]{2,1,0:T(8,128)(2,1)} %param.6) | copy-start | bytes 3145732

commit v2 on v1

--- a/solution.py
+++ b/solution.py
@@ -241,7 +241,8 @@
 MESH = pl.DeviceIdType.MESH
 GROUP = 1
 LAG = 10
-AHEAD = 3
+AHEAD = 1
+PACE = 1
 NT = (((1,), (1,)), ((), ()))
 TN = (((0,), (0,)), ((), ()))
 NN = (((1,), (0,)), ((), ()))
@@ -446,8 +447,8 @@
             dv[:, cc] = (acc[1, :, cc] + lb[1, :, cc].astype(jnp.float32)).astype(bf)
             return carry
 
+        drain(1, 0)
         lax.fori_loop(0, chunks, finish, 0)
-        drain(1, 0)
         mine.wait_send()
         total_out()
 
@@ -569,16 +570,26 @@
         def send(c, carry):
             for kind, src in enumerate((q, k, v, g)):
                 to_left(src.at[:, cols(c)], lb.at[kind, :, cols(c)], kind // 2, c).start()
-            return carry
+
+            @pl.when(c >= PACE)
+            def _():
+                sent(c - PACE)
+
+            return carry
+
+        def sent(c):
+            for pair in range(2):
+                to_left(both(lb, pair, c), both(lb, pair, c), pair, c).wait_send()
 
         lax.fori_loop(0, chunks, send, 0)
+        for c in range(max(chunks - PACE, 0), chunks):
+            sent(c)
 
         def collect(c, carry):
             wait_right(2, c)
             return carry
 
         lax.fori_loop(0, chunks, collect, 0)
-        drain(0, 2)
         total_out()
 
 
@@ -623,7 +634,7 @@
             pltpu.SemaphoreType.DMA((4,)),
         ],
         compiler_params=pltpu.CompilerParams(
-            collective_id=0, has_side_effects=True, vmem_limit_bytes=48 * 1024 * 1024
+            collective_id=0, has_side_effects=True, vmem_limit_bytes=96 * 512 * 1024
         ),
     )(
         layout.transpose(1, 2, 0),

time: 117 us -> 115 us (0.983)
  Pallas kernels: 114 us -> 112 us
    pallas_call x1, Pallas kernels: 112 us -> 110 us  [body(): pl.pallas_call(functools.partial(line_kernel, heads, dps), out_shape=(fla...]
where the time goes in v2:
time: 115 us
  Pallas kernels  112 us (97%)
  local copies, waits for them, and re-layouts  1.91 us (2%)
    pallas_call x1, Pallas kernels, body(): pl.pallas_call(functools.partial(line_kernel, heads, dps), out_shape=(fla...  110 us

profile of v2, /device:TPU:0, one launch (start us, length us, event | category | flops | bytes accessed | tf_op | source)
XLA Modules:
  0.0 114.8 jit_solution(14382110500648914048)
XLA Ops:
  0.6 0.0 copy-start.1
  0.6 0.0 copy-start.2
  0.7 0.7 copy-done.1
  1.3 0.0 copy-done.2
  1.3 0.0 copy-start
  1.3 1.2 %copy-done = bf16[1,128,4096]{2,1,0:T(8,128)(2,1)S(1)} copy-done((bf16[1,128,4096]{2,1,0:T(8,128)(2,1)S(1)}, bf16[1,128,4096]{2,1,0:T(8,128)(2,1)}, u32[]{:S(2)}) %copy-start) | copy-done | bytes 1048600
  2.6 109.6 %shard_map.101 = (bf16[128,4096]{1,0:T(8,128)(2,1)S(1)}, bf16[128,4096]{1,0:T(8,128)(2,1)S(1)}, bf16[128,4096]{1,0:T(8,128)(2,1)S(1)}, bf16[128,4096]{1,0:T(8,128)(2,1)S(1)}, f32[32,128]{1,0:T(8,128)S(1)}) custom-call(s32[4,4,32]{2,1,0:T(4,128)S(1)} %bitcast.10, f32[32]{0:T(128)S(1)} %copy-done.2, bf16[128,4096]{1,0:T(8,128)(2,1)S(1)} %bitcast.9, ...), custom_call_target="tpu_custom_call" | custom-call | tf_op jit(solution)/shard_map/pallas_call | solution.py:619
  112.2 2.0 %shard_map.102 = (bf16[128,4096]{1,0:T(8,128)(2,1)}, bf16[128,4096]{1,0:T(8,128)(2,1)}, bf16[128,4096]{1,0:T(8,128)(2,1)}, bf16[128,4096]{1,0:T(8,128)(2,1)}) custom-call(bf16[128,4096]{1,0:T(8,128)(2,1)S(1)} %get-tuple-element.14.refs_0_, bf16[128,4096]{1,0:T(8,128)(2,1)S(1)} %get-tuple-element.15.refs_1_, bf16[128,4096]{1,0:T(8,128)(2,1)S(1)} %get-tuple-element.16.refs_2_, ...), custom_call_target="tpu_custom_call" | custom-call | tf_op jit(solution)/shard_map/pallas_call | solution.py:644
  114.2 0.6 reduce_sum.9
Async XLA Ops:
  0.6 0.7 copy-start.1
  0.6 0.7 copy-start.2
  1.3 1.2 %copy-start = (bf16[1,128,4096]{2,1,0:T(8,128)(2,1)S(1)}, bf16[1,128,4096]{2,1,0:T(8,128)(2,1)}, u32[]{:S(2)}) copy-start(bf16[1,128,4096]{2,1,0:T(8,128)(2,1)} %param.6) | copy-start | bytes 3145732
